TPU v7x, 128 devices: a whole 4x4x4 slice. The times are simulated.
128 devices in a mesh: row: 8 (over z, core), col: 16 (over y, x).
Axes of the slice: x: 4, y: 4, z: 4, core: 2. Of those that a mesh axis runs over, the one named last changes fastest.
Arguments:
- image: float32 [32, 32, 64, 128], P('row', 'col'), may hold values from -6 to 6
- u_factors: bfloat16 [40, 64, 1024, 256], P('row', 'col'), may hold values from -0.0625 to 0.0625
- v_factors: bfloat16 [40, 64, 1024, 256], P('row', 'col'), may hold values from -0.1875 to 0.1875
- ranks: int32 [40, 64], P('row', 'col'), may hold values from 16 to 256
- measured: bfloat16 [40960, 128], P('row'), may hold values from -6 to 6
Outputs:
- new_image: float32 [32, 32, 64, 128], P('row', 'col')
All inputs are finite; a program needn't handle non-finite values.
Results may differ from a plain program's by a relative error of at most 0.0051.
Values may be sent and summed in bfloat16 or wider, within the bound.
A program may use at most 128 MiB of HBM per device.

v0:
```python
import jax
import jax.numpy as jnp
from jax import lax
from jax.sharding import PartitionSpec as P

diff_rate = 0.12
edge_scale = 0.5


def padded_2(block, sides, width):
    for axis, dim in sides:
        count = lax.axis_size(axis)
        forward = [(i, i + 1) for i in range(count - 1)]
        backward = [(target, source) for source, target in forward]
        low = lax.ppermute(
            lax.slice_in_dim(block, block.shape[dim] - width, None, axis=dim), axis, forward
        )
        high = lax.ppermute(lax.slice_in_dim(block, 0, width, axis=dim), axis, backward)
        block = jnp.concatenate([low, block, high], axis=dim)
    return block


def flux(delta):
    scaled = delta / edge_scale
    return delta / (1.0 + scaled * scaled)


def diffuse_margin(extended):
    padded = jnp.pad(extended, ((0, 0), (0, 0), (1, 1), (0, 0)))
    center = padded[1:-1, 1:-1, 1:-1]
    total = flux(padded[2:, 1:-1, 1:-1] - center) + flux(padded[:-2, 1:-1, 1:-1] - center)
    total = total + flux(padded[1:-1, 2:, 1:-1] - center) + flux(padded[1:-1, :-2, 1:-1] - center)
    total = total + flux(padded[1:-1, 1:-1, 2:] - center) + flux(padded[1:-1, 1:-1, :-2] - center)
    return center + diff_rate * total


def body(image, u_factors, v_factors, ranks, measured):
    row_tiles, col_tiles, tile_len, rank_max = u_factors.shape
    frames = image.shape[3]
    whole = lax.all_gather(image.astype(jnp.bfloat16), "row", axis=0, tiled=True)
    xtiles = whole.reshape(col_tiles, tile_len, frames)
    levels = lax.broadcasted_iota(jnp.int32, (row_tiles, col_tiles, rank_max), 2)
    mask = (levels < ranks[:, :, None]).astype(jnp.float32)
    coef = jnp.einsum("ijkr,jkf->ijrf", v_factors, xtiles, preferred_element_type=jnp.float32)
    coef = (coef * mask[:, :, :, None]).astype(jnp.bfloat16)
    partial_value = jnp.einsum(
        "ijkr,ijrf->ikf", u_factors, coef, preferred_element_type=jnp.float32
    )
    partial_value = partial_value.reshape(row_tiles * tile_len, frames)
    total = lax.psum(partial_value, "col")
    resid = (total - measured.astype(jnp.float32)).astype(jnp.bfloat16)
    resid = resid.reshape(row_tiles, tile_len, frames)
    back = jnp.einsum("ijkr,ikf->ijrf", u_factors, resid, preferred_element_type=jnp.float32)
    back = (back * mask[:, :, :, None]).astype(jnp.bfloat16)
    grad_terms = jnp.einsum("ijkr,ijrf->jkf", v_factors, back, preferred_element_type=jnp.float32)
    grad_terms = grad_terms.reshape(col_tiles * tile_len, frames)
    gradient = lax.psum_scatter(grad_terms, "row", scatter_dimension=0, tiled=True)
    moved = image - gradient.reshape(image.shape)
    for step in range(2):
        extended = padded_2(moved, (("row", 0), ("col", 1)), 1)
        moved = diffuse_margin(extended)
    return moved


def solution(mesh):
    placed = (
        P("row", "col", None, None),
        P("row", "col", None, None),
        P("row", "col", None, None),
        P("row", "col"),
        P("row", None),
    )
    return jax.shard_map(
        body, mesh=mesh, in_specs=placed, out_specs=P("row", "col", None, None), check_vma=False
    )
```

profile of v0, /device:TPU:25, one launch (start us, length us, event | category | flops | bytes accessed | tf_op | source)
XLA Modules:
  0.0 237.7 jit_solution(13111002786819206620)
XLA Ops:
  6.5 0.0 all-gather.2.cloned.1.call-start
  6.5 1.6 convert_element_type.28
  8.2 0.0 all-gather.2.cloned.1.call-update
  8.2 0.0 all-reduce.4.cloned.1.call-start
  8.2 0.8 copy.20
  9.0 0.1 fusion.25
  9.1 26.1 %all-gather.2.cloned.1.call-done = bf16[32,2,64,128]{3,2,1,0:T(8,128)(2,1)} async-done(((bf16[4,2,64,128]{3,2,1,0:T(8,128)(2,1)}), bf16[32,2,64,128]{3,2,1,0:T(8,128)(2,1)}) %all-gather.2.cloned.1.call-update) | async-done | bytes 1048592 | tf_op jit(solution)/shard_map/all_gather | solution.py:40
  35.2 11.8 %convolution_bitcast_fusion = f32[5,1024,128]{1,2,0:T(8,128)S(1)} fusion(bf16[5,4,1024,256]{3,2,1,0:T(8,128)(2,1)} %param.6, bf16[4,1024,128,1]{2,1,0,3:T(8,128)(2,1)} %bitcast.33, bf16[5,4,1024,256]{3,2,1,0:T(8,128)(2,1)} %param.7, f32[5,4,256]{2,1,0:T(4,128)S(1)} %fusion.25), kind=kOutput, calls=%fused_computation.8 | convolution fusion | flops 2685665280 | bytes 24662016 | tf_op jit(solution)/shard_map/ijkr,ijrf->ikf/dot_general | solution.py:46
  47.0 2.1 copy.21
  49.1 0.0 copy-start
  49.1 0.0 all-reduce.4.cloned.1.call-update
  49.2 0.0 reduce-scatter.2.cloned.1.call-start
  49.2 90.6 %all-reduce.4.cloned.1.call-done = f32[5120,128]{1,0:T(8,128)} async-done(((f32[5120,128]{1,0:T(8,128)}), f32[5120,128]{1,0:T(8,128)}) %all-reduce.4.cloned.1.call-update) | async-done | bytes 2621456 | tf_op jit(solution)/shard_map/psum | solution.py:50
  139.8 0.0 copy-done
  139.8 2.0 subtract_convert_fusion
  141.8 9.7 %fusion.7 = f32[4,1024,128]{1,2,0:T(8,128)S(1)} fusion(bf16[5,4,1024,256]{3,2,1,0:T(8,128)(2,1)} %param.7, bf16[5,1024,128,1]{2,1,0,3:T(8,128)(2,1)S(1)} %bitcast.36, bf16[5,4,1024,256]{3,2,1,0:T(8,128)(2,1)} %param.6, f32[5,4,256]{2,0,1:T(8,128)S(1)} %copy.24), kind=kOutput, calls=%fused_computation.9 | convolution fusion | flops 2685665280 | bytes 24399872 | tf_op jit(solution)/shard_map/ijkr,ijrf->jkf/dot_general | solution.py:55
  151.5 0.0 copy-start.1
  151.5 1.8 copy.26
  153.4 0.0 reduce-scatter.2.cloned.1.call-update
  153.4 31.9 %reduce-scatter.2.cloned.1.call-done = f32[512,128]{1,0:T(8,128)} async-done(((f32[4096,128]{1,0:T(8,128)}), f32[512,128]{1,0:T(8,128)}) %reduce-scatter.2.cloned.1.call-update) | async-done | bytes 262160 | tf_op jit(solution)/shard_map/reduce_scatter | solution.py:57
  185.3 0.0 copy-done.1
  185.3 1.0 sub.43
  186.3 5.6 %collective-permute-start = (f32[1,2,64,128]{3,2,1,0:T(8,128)S(1)}, f32[1,2,64,128]{3,2,1,0:T(8,128)S(1)}, u32[]{:S(2)}, u32[]{:S(2)}) collective-permute-start(f32[1,2,64,128]{3,2,1,0:T(8,128)S(1)} %get-tuple-element.12), channel_id=1, source_target_pairs={{16,0},{32,16},{48,32},{64,48},{80,64},{96,80},{112,96},{17,1},{33... | collective-permute-start | bytes 196616 | tf_op jit(solution)/shard_map/ppermute | solution.py:18
  192.0 1.9 collective-permute-start.1
  193.9 0.0 collective-permute-done
  193.9 1.3 collective-permute-done.1
  195.3 4.5 %collective-permute-start.2 = (f32[6,1,64,128]{3,2,1,0:T(8,128)S(1)}, f32[6,1,64,128]{3,2,1,0:T(8,128)S(1)}, u32[]{:S(2)}, u32[]{:S(2)}) collective-permute-start(f32[6,1,64,128]{3,2,1,0:T(8,128)S(1)} %get-tuple-element.8), channel_id=1, source_target_pairs={{1,0},{2,1},{3,2},{4,3},{5,4},{6,5},{7,6},{8,7},{9,8},{10,9},{11,1... | collective-permute-start | bytes 589832 | tf_op jit(solution)/shard_map/ppermute | solution.py:18
  199.8 1.9 collective-permute-start.3
  201.7 2.3 collective-permute-done.2
  204.0 5.9 %collective-permute-done.3 = f32[6,1,64,128]{3,2,1,0:T(8,128)S(1)} collective-permute-done((f32[6,1,64,128]{3,2,1,0:T(8,128)S(1)}, f32[6,1,64,128]{3,2,1,0:T(8,128)S(1)}, u32[]{:S(2)}, u32[]{:S(2)}) %collective-permute-start.3) | collective-permute-done | bytes 196640 | tf_op jit(solution)/shard_map/ppermute | solution.py:15
  209.9 0.1 select_maximum_fusion.4
  210.0 0.4 multiply_add_fusion.1
  210.5 3.1 %collective-permute-start.4 = (f32[1,2,64,128]{3,2,1,0:T(8,128)S(1)}, f32[1,2,64,128]{3,2,1,0:T(8,128)S(1)}, u32[]{:S(2)}, u32[]{:S(2)}) collective-permute-start(f32[1,2,64,128]{3,2,1,0:T(8,128)S(1)} %get-tuple-element.10), channel_id=1, source_target_pairs={{16,0},{32,16},{48,32},{64,48},{80,64},{96,80},{112,96},{17,1},{33... | collective-permute-start | bytes 196616 | tf_op jit(solution)/shard_map/ppermute | solution.py:18
  213.6 2.9 %collective-permute-start.5 = (f32[1,2,64,128]{3,2,1,0:T(8,128)S(1)}, f32[1,2,64,128]{3,2,1,0:T(8,128)S(1)}, u32[]{:S(2)}, u32[]{:S(2)}) collective-permute-start(f32[1,2,64,128]{3,2,1,0:T(8,128)S(1)} %get-tuple-element.9), channel_id=1, source_target_pairs={{0,16},{16,32},{32,48},{48,64},{64,80},{80,96},{96,112},{1,17},{17... | collective-permute-start | bytes 196616 | tf_op jit(solution)/shard_map/ppermute | solution.py:15
  216.5 0.0 collective-permute-done.4
  216.5 1.3 collective-permute-done.5
  217.9 1.9 collective-permute-start.6
  219.8 3.4 %collective-permute-start.7 = (f32[6,1,64,128]{3,2,1,0:T(8,128)S(1)}, f32[6,1,64,128]{3,2,1,0:T(8,128)S(1)}, u32[]{:S(2)}, u32[]{:S(2)}) collective-permute-start(f32[6,1,64,128]{3,2,1,0:T(8,128)S(1)} %get-tuple-element.5), channel_id=1, source_target_pairs={{0,1},{1,2},{2,3},{3,4},{4,5},{5,6},{6,7},{7,8},{8,9},{9,10},{10,1... | collective-permute-start | bytes 589832 | tf_op jit(solution)/shard_map/ppermute | solution.py:15
  223.2 3.1 %collective-permute-done.6 = f32[6,1,64,128]{3,2,1,0:T(8,128)S(1)} collective-permute-done((f32[6,1,64,128]{3,2,1,0:T(8,128)S(1)}, f32[6,1,64,128]{3,2,1,0:T(8,128)S(1)}, u32[]{:S(2)}, u32[]{:S(2)}) %collective-permute-start.6) | collective-permute-done | bytes 196640 | tf_op jit(solution)/shard_map/ppermute | solution.py:18
  226.2 3.7 %collective-permute-done.7 = f32[6,1,64,128]{3,2,1,0:T(8,128)S(1)} collective-permute-done((f32[6,1,64,128]{3,2,1,0:T(8,128)S(1)}, f32[6,1,64,128]{3,2,1,0:T(8,128)S(1)}, u32[]{:S(2)}, u32[]{:S(2)}) %collective-permute-start.7) | collective-permute-done | bytes 196640 | tf_op jit(solution)/shard_map/ppermute | solution.py:15
  230.0 0.1 select_maximum_fusion
  230.1 1.1 multiply_add_fusion
  (7 shorter events, 0.1 us)
Async XLA Ops:
  6.5 28.7 %all-gather.2.cloned.1.call-start = ((), (), s32[]{:S(2)}) async-start(), calls=%async_computation.1 | async-start | bytes 1179648 | tf_op jit(solution)/shard_map/all_gather | solution.py:40
  8.2 131.6 %all-reduce.4.cloned.1.call-start = ((), (), s32[]{:S(2)}) async-start(), calls=%async_computation.2 | async-start | bytes 5242880 | tf_op jit(solution)/shard_map/psum | solution.py:50
  49.1 90.7 %copy-start = (bf16[5120,128]{1,0:T(8,128)(2,1)S(1)}, bf16[5120,128]{1,0:T(8,128)(2,1)}, u32[]{:S(2)}) copy-start(bf16[5120,128]{1,0:T(8,128)(2,1)} %param.9) | copy-start | bytes 3932164
  49.2 136.2 %reduce-scatter.2.cloned.1.call-start = ((), (), s32[]{:S(2)}) async-start(), calls=%async_computation.3 | async-start | bytes 2359296 | tf_op jit(solution)/shard_map/reduce_scatter | solution.py:57
  151.5 33.8 %copy-start.1 = (f32[4,2,64,128]{3,2,1,0:T(8,128)S(1)}, f32[4,2,64,128]{3,2,1,0:T(8,128)}, u32[]{:S(2)}) copy-start(f32[4,2,64,128]{3,2,1,0:T(8,128)} %param.5) | copy-start | bytes 786436
  186.3 7.6 %collective-permute-start = (f32[1,2,64,128]{3,2,1,0:T(8,128)S(1)}, f32[1,2,64,128]{3,2,1,0:T(8,128)S(1)}, u32[]{:S(2)}, u32[]{:S(2)}) collective-permute-start(f32[1,2,64,128]{3,2,1,0:T(8,128)S(1)} %get-tuple-element.12), channel_id=1, source_target_pairs={{16,0},{32,16},{48,32},{64,48},{80,64},{96,80},{112,96},{17,1},{33... | collective-permute-start | bytes 196616 | tf_op jit(solution)/shard_map/ppermute | solution.py:18
  192.0 3.2 %collective-permute-start.1 = (f32[1,2,64,128]{3,2,1,0:T(8,128)S(1)}, f32[1,2,64,128]{3,2,1,0:T(8,128)S(1)}, u32[]{:S(2)}, u32[]{:S(2)}) collective-permute-start(f32[1,2,64,128]{3,2,1,0:T(8,128)S(1)} %get-tuple-element.11), channel_id=1, source_target_pairs={{0,16},{16,32},{32,48},{48,64},{64,80},{80,96},{96,112},{1,17},{17... | collective-permute-start | bytes 196616 | tf_op jit(solution)/shard_map/ppermute | solution.py:15
  195.3 8.8 %collective-permute-start.2 = (f32[6,1,64,128]{3,2,1,0:T(8,128)S(1)}, f32[6,1,64,128]{3,2,1,0:T(8,128)S(1)}, u32[]{:S(2)}, u32[]{:S(2)}) collective-permute-start(f32[6,1,64,128]{3,2,1,0:T(8,128)S(1)} %get-tuple-element.8), channel_id=1, source_target_pairs={{1,0},{2,1},{3,2},{4,3},{5,4},{6,5},{7,6},{8,7},{9,8},{10,9},{11,1... | collective-permute-start | bytes 589832 | tf_op jit(solution)/shard_map/ppermute | solution.py:18
  199.8 10.1 %collective-permute-start.3 = (f32[6,1,64,128]{3,2,1,0:T(8,128)S(1)}, f32[6,1,64,128]{3,2,1,0:T(8,128)S(1)}, u32[]{:S(2)}, u32[]{:S(2)}) collective-permute-start(f32[6,1,64,128]{3,2,1,0:T(8,128)S(1)} %get-tuple-element.7), channel_id=1, source_target_pairs={{0,1},{1,2},{2,3},{3,4},{4,5},{5,6},{6,7},{7,8},{8,9},{9,10},{10,1... | collective-permute-start | bytes 589832 | tf_op jit(solution)/shard_map/ppermute | solution.py:15
  210.5 6.0 %collective-permute-start.4 = (f32[1,2,64,128]{3,2,1,0:T(8,128)S(1)}, f32[1,2,64,128]{3,2,1,0:T(8,128)S(1)}, u32[]{:S(2)}, u32[]{:S(2)}) collective-permute-start(f32[1,2,64,128]{3,2,1,0:T(8,128)S(1)} %get-tuple-element.10), channel_id=1, source_target_pairs={{16,0},{32,16},{48,32},{64,48},{80,64},{96,80},{112,96},{17,1},{33... | collective-permute-start | bytes 196616 | tf_op jit(solution)/shard_map/ppermute | solution.py:18
  213.6 4.2 %collective-permute-start.5 = (f32[1,2,64,128]{3,2,1,0:T(8,128)S(1)}, f32[1,2,64,128]{3,2,1,0:T(8,128)S(1)}, u32[]{:S(2)}, u32[]{:S(2)}) collective-permute-start(f32[1,2,64,128]{3,2,1,0:T(8,128)S(1)} %get-tuple-element.9), channel_id=1, source_target_pairs={{0,16},{16,32},{32,48},{48,64},{64,80},{80,96},{96,112},{1,17},{17... | collective-permute-start | bytes 196616 | tf_op jit(solution)/shard_map/ppermute | solution.py:15
  217.9 8.4 %collective-permute-start.6 = (f32[6,1,64,128]{3,2,1,0:T(8,128)S(1)}, f32[6,1,64,128]{3,2,1,0:T(8,128)S(1)}, u32[]{:S(2)}, u32[]{:S(2)}) collective-permute-start(f32[6,1,64,128]{3,2,1,0:T(8,128)S(1)} %get-tuple-element.6), channel_id=1, source_target_pairs={{1,0},{2,1},{3,2},{4,3},{5,4},{6,5},{7,6},{8,7},{9,8},{10,9},{11,1... | collective-permute-start | bytes 589832 | tf_op jit(solution)/shard_map/ppermute | solution.py:18
  219.8 10.2 %collective-permute-start.7 = (f32[6,1,64,128]{3,2,1,0:T(8,128)S(1)}, f32[6,1,64,128]{3,2,1,0:T(8,128)S(1)}, u32[]{:S(2)}, u32[]{:S(2)}) collective-permute-start(f32[6,1,64,128]{3,2,1,0:T(8,128)S(1)} %get-tuple-element.5), channel_id=1, source_target_pairs={{0,1},{1,2},{2,3},{3,4},{4,5},{5,6},{6,7},{7,8},{8,9},{9,10},{10,1... | collective-permute-start | bytes 589832 | tf_op jit(solution)/shard_map/ppermute | solution.py:15
Sparse Core Ops, SparseCore 0:
  9.1 26.1 all-gather.1
  49.3 90.4 all-reduce.3
  153.5 31.7 reduce-scatter.1
where the time goes:
time: 238 us
  waiting for transfers between devices  166 us (70%)
  starting transfers between devices  25.4 us (11%)
  matrix products  21.5 us (9%)
  between operations  13.3 us (6%)
  other arithmetic  6.4 us (3%)
  local copies, waits for them, and re-layouts  4.83 us (2%)
    psum x1, waiting for transfers between devices, body(): total = lax.psum(partial_value, 'col')  90.6 us
    reduce_scatter x1, waiting for transfers between devices, body(): lax.psum_scatter(grad_terms, 'row', scatter_dimension=0, tiled=True)  31.9 us
    all_gather x1, waiting for transfers between devices, body(): lax.all_gather(image.astype(jnp.bfloat16), 'row', axis=0, tiled=True)  26.1 us
    ppermute x4, starting transfers between devices, padded_2(): lax.ppermute(lax.slice_in_dim(block, 0, width, axis=dim), axis, backward)  15.2 us
    ppermute x4, waiting for transfers between devices, padded_2(): lax.ppermute(lax.slice_in_dim(block, block.shape[dim] - width, None, axis...  12.2 us
    dot_general x1, matrix products, body(): jnp.einsum('ijkr,ijrf->ikf', u_factors, coef, preferred_element_type=jnp....  11.8 us
    ppermute x4, starting transfers between devices, padded_2(): lax.ppermute(lax.slice_in_dim(block, block.shape[dim] - width, None, axis...  10.1 us
    dot_general x1, matrix products, body(): jnp.einsum('ijkr,ijrf->jkf', v_factors, back, preferred_element_type=jnp....  9.72 us
  transfers between devices with their start and end apart: 11, of which 9 were waited for; matrix products, arithmetic and copies ran while one was open for 0% of the time, Pallas kernels for 0%

commit v1 on v0

v1 whole, which is shorter than its diff:
```python
import jax
import jax.numpy as jnp
from jax import lax
from jax.experimental import pallas as pl
from jax.experimental.pallas import tpu as pltpu
from jax.sharding import PartitionSpec as P

MESH = pl.DeviceIdType.MESH
NT = (((1,), (1,)), ((), ()))
BF = jnp.bfloat16
F32 = jnp.float32

LAG_RELAY, LAG_SUM, LAG_RESID, LAG_SPREAD, LAG_FORWARD, LAG_BACK = 2, 4, 6, 8, 10, 12


class Copy:
    def __init__(self, src, dst, ss, rs, dev):
        self.parts = (src, dst, ss, rs, dev)

    def made(self):
        src, dst, (ss, si), (rs, ri), dev = self.parts
        return pltpu.make_async_remote_copy(
            src_ref=at(src), dst_ref=at(dst), send_sem=ss.at[si], recv_sem=rs.at[ri], device_id=dev, device_id_type=MESH)

    def start(self):
        self.made().start()

    def wait_recv(self):
        self.made().wait_recv()

    def wait_send(self):
        self.made().wait_send()


def at(place):
    if not isinstance(place, tuple):
        return place
    ref, *index = place
    return ref.at[tuple(index)]


def flux(d):
    return d / (1.0 + 4.0 * (d * d))


def kernel(
    img_hbm, u_hbm, v_hbm, ranks, meas_hbm, out,
    img, u, v, mb, mt, xt, coef,
    ps, d2, qb, r1, sums, ph2, r2, rt,
    grad, cs, cr, zs, zd, zr, moved, m16, hr, hc, hx, s1,
    lsem, ax_s, ax_r, ex_s, ex_r, gc_s, gc_r, gz_s, gz_r, hs_s, hs_r,
):
    n_i = u.shape[0]
    r = lax.axis_index("row")
    c = lax.axis_index("col")
    z, h = r // 2, r % 2
    y, x = c // 4, c % 4
    zp, zm, zf = (z + 1) % 4, (z + 3) % 4, (z + 2) % 4
    order = (z, zm, zp, zf)

    img_copy = pltpu.make_async_copy(img_hbm, img, lsem.at[0])
    img_copy.start()
    v_copies = [pltpu.make_async_copy(v_hbm.at[:, order[k]], v.at[:, k], lsem.at[1 + k]) for k in range(4)]
    u_copies = [pltpu.make_async_copy(u_hbm.at[:, order[k]], u.at[:, k], lsem.at[5 + k]) for k in range(4)]
    m_copies = [pltpu.make_async_copy(meas_hbm.at[:, 0, x], mb.at[0], lsem.at[9]),
                pltpu.make_async_copy(meas_hbm.at[:, 1, y], mb.at[1], lsem.at[10])]

    def at_z(zz, hh=h):
        return (zz * 2 + hh, c)

    sibling = at_z(z, 1 - h)
    rp, rm = (r + 1) % 8, (r + 7) % 8
    cp, cm = (c + 1) % 16, (c + 15) % 16

    def along_x(pos):
        return (r, y * 4 + pos)

    def along_y(pos):
        return (r, pos * 4 + x)

    peers = [sibling, at_z(zp), at_z(zm)]
    peers += [along_x((x + d) % 4) for d in (1, 2, 3)] + [along_y((y + d) % 4) for d in (1, 2, 3)]
    peers += [(rp, c), (rm, c), (r, cp), (r, cm), (rp, cp), (rp, cm), (rm, cp), (rm, cm)]
    barrier = pltpu.get_barrier_semaphore()
    for peer in peers:
        pl.semaphore_signal(barrier, inc=1, device_id=peer, device_id_type=MESH)

    img_copy.wait()
    v_copies[0].start()
    for k in (1, 2, 3):
        v_copies[k].start()
    for m in m_copies:
        m.start()
    for k in range(4):
        u_copies[k].start()
    xt[r] = img[...].T.astype(BF)
    pl.semaphore_wait(barrier, len(peers))

    lo, hi = pl.ds(0, 64), pl.ds(64, 64)

    def xcopy(i, blk, part, dev):
        ref = (xt, blk) if part is None else (xt, blk, part)
        return Copy(ref, ref, (ax_s, i), (ax_r, i), dev)

    b0, bm, bp, bf = r, zm * 2 + h, zp * 2 + h, zf * 2 + h
    o0, om, op, of = z * 2 + 1 - h, zm * 2 + 1 - h, zp * 2 + 1 - h, zf * 2 + 1 - h
    out_x = [
        xcopy(0, b0, None, sibling),
        xcopy(1, b0, lo, at_z(zp)), xcopy(2, b0, hi, at_z(zm)), xcopy(3, b0, hi, at_z(zp)), xcopy(4, b0, lo, at_z(zm)),
        xcopy(5, bm, lo, at_z(zp)), xcopy(6, bp, hi, at_z(zm)),
        xcopy(7, bm, lo, sibling), xcopy(8, bp, hi, sibling), xcopy(9, bm, hi, sibling), xcopy(10, bp, lo, sibling),
        xcopy(11, bf, lo, sibling), xcopy(12, bf, hi, sibling),
    ]
    in_x = [
        xcopy(0, o0, None, sibling),
        xcopy(1, bm, lo, sibling), xcopy(2, bp, hi, sibling), xcopy(3, bm, hi, sibling), xcopy(4, bp, lo, sibling),
        xcopy(5, bf, lo, sibling), xcopy(6, bf, hi, sibling),
        xcopy(7, om, lo, sibling), xcopy(8, op, hi, sibling), xcopy(9, om, hi, sibling), xcopy(10, op, lo, sibling),
        xcopy(11, of, lo, sibling), xcopy(12, of, hi, sibling),
    ]
    for i in (1, 2, 0, 3, 4):
        out_x[i].start()

    lane = lax.broadcasted_iota(jnp.int32, (128, 256), 1)

    def masked(value, i, k):
        return jnp.where(lane < ranks[order[k], i], value, 0.0).astype(BF)

    def coefs(k):
        v_copies[k].wait()

        def one(i, _):
            j = order[k]
            xj = jnp.concatenate([xt[2 * j], xt[2 * j + 1]], axis=1)
            coef[i, k] = masked(jnp.dot(xj, v[i, k], preferred_element_type=F32), i, k)
            return 0

        lax.fori_loop(0, n_i, one, 0)

    in_x[0].wait_recv()
    coefs(0)
    in_x[1].wait_recv()
    out_x[5].start()
    out_x[7].start()
    in_x[2].wait_recv()
    out_x[6].start()
    out_x[8].start()
    for m in m_copies:
        m.wait()

    def turn(i, _):
        for ax in (0, 1):
            mt[i, ax] = mb[ax, i].astype(F32).T
        return 0

    lax.fori_loop(0, n_i, turn, 0)
    in_x[3].wait_recv()
    out_x[9].start()
    in_x[4].wait_recv()
    out_x[10].start()
    in_x[7].wait_recv()
    in_x[9].wait_recv()
    coefs(1)
    in_x[8].wait_recv()
    in_x[10].wait_recv()
    coefs(2)
    in_x[5].wait_recv()
    out_x[11].start()
    in_x[6].wait_recv()
    out_x[12].start()
    in_x[11].wait_recv()
    in_x[12].wait_recv()
    coefs(3)
    for k in range(4):
        u_copies[k].wait()

    axes = (
        (0, x, along_x, y, along_y),
        (4, y, along_y, x, along_x),
    )

    def exch(i, ax):
        base, p, dev1, s, dev2 = axes[ax]
        pp, pm, pf = (p + 1) % 4, (p + 3) % 4, (p + 2) % 4

        def cpy(n, src, dst, dev):
            return Copy(src, dst, (ex_s, (i, ax, n)), (ex_r, (i, ax, n)), dev)

        def piece(pos):
            return pl.ds(pl.multiple_of(pos * 32, 32), 32)

        own = (rt, i, base + p)
        sends = [
            cpy(0, (ps, i, base + pf, lo), (d2, i, ax, 0), dev1(pp)),
            cpy(1, (ps, i, base + pf, hi), (d2, i, ax, 1), dev1(pm)),
            cpy(2, (ps, i, base + pp, hi), (r1, i, ax, 0, hi), dev1(pp)),
            cpy(3, (ps, i, base + pm, lo), (r1, i, ax, 1, lo), dev1(pm)),
            cpy(4, (qb, i, ax, 0), (r1, i, ax, 0, lo), dev1(pp)),
            cpy(5, (qb, i, ax, 1), (r1, i, ax, 1, hi), dev1(pm)),
        ]
        for d in (1, 2, 3):
            sends.append(cpy(5 + d, (ph2, i, ax, piece((s + d) % 4)), (r2, i, ax, d - 1), dev2((s + d) % 4)))
        for d in (1, 2, 3):
            sends.append(cpy(8 + d, own + (piece(s),), own + (piece(s),), dev2((s + d) % 4)))
        sends += [
            cpy(12, own + (lo,), own + (lo,), dev1(pp)),
            cpy(13, own + (hi,), own + (hi,), dev1(pm)),
            cpy(14, own + (hi,), own + (hi,), dev1(pp)),
            cpy(15, own + (lo,), own + (lo,), dev1(pm)),
            cpy(16, (rt, i, base + pm, lo), (rt, i, base + pm, lo), dev1(pp)),
            cpy(17, (rt, i, base + pp, hi), (rt, i, base + pp, hi), dev1(pm)),
        ]
        lands = [(d2, i, ax, 0), (d2, i, ax, 1), (r1, i, ax, 0, hi), (r1, i, ax, 1, lo), (r1, i, ax, 0, lo), (r1, i, ax, 1, hi)]
        lands += [(r2, i, ax, d - 1) for d in (1, 2, 3)]
        lands += [own + (piece((s + 4 - d) % 4),) for d in (1, 2, 3)]
        lands += [(rt, i, base + pm, lo), (rt, i, base + pp, hi), (rt, i, base + pm, hi), (rt, i, base + pp, lo),
                  (rt, i, base + pf, lo), (rt, i, base + pf, hi)]

        def wait(*ns):
            for n in ns:
                cpy(n, lands[n], lands[n], dev1(pp)).wait_recv()

        return sends, wait, base, p, pp, pm, s, piece

    def stage_pred(i):
        cf = [coef[i, k] for k in range(4)]
        for q in range(4):
            rows = slice(256 * q, 256 * q + 256)
            total = lax.dot_general(cf[0], u[i, 0, rows], NT, preferred_element_type=F32)
            for k in (1, 2, 3):
                total += lax.dot_general(cf[k], u[i, k, rows], NT, preferred_element_type=F32)
            ps[i, 2 * q] = total[:, :128].astype(BF)
            ps[i, 2 * q + 1] = total[:, 128:].astype(BF)
        both = [exch(i, ax)[0] for ax in (0, 1)]
        for n in range(4):
            for sends in both:
                sends[n].start()

    def stage_relay(i):
        for ax in (0, 1):
            sends, wait, base, p, pp, pm, s, piece = exch(i, ax)
            wait(0)
            qb[i, ax, 0] = (ps[i, base + pp, :64].astype(F32) + d2[i, ax, 0].astype(F32)).astype(BF)
            sends[4].start()
            wait(1)
            qb[i, ax, 1] = (ps[i, base + pm, 64:].astype(F32) + d2[i, ax, 1].astype(F32)).astype(BF)
            sends[5].start()

    def stage_sum(i):
        for ax in (0, 1):
            sends, wait, base, p, pp, pm, s, piece = exch(i, ax)
            wait(2, 3, 4, 5)
            total = ps[i, base + p].astype(F32) + r1[i, ax, 0].astype(F32) + r1[i, ax, 1].astype(F32)
            sums[i, ax] = total
            ph2[i, ax] = total.astype(BF)
            for n in (7, 6, 8):
                sends[n].start()

    def stage_resid(i):
        for ax in (0, 1):
            sends, wait, base, p, pp, pm, s, piece = exch(i, ax)
            wait(6, 7, 8)
            total = sums[i, ax, piece(s)]
            for d in range(3):
                total += r2[i, ax, d].astype(F32)
            rt[i, base + p, piece(s)] = (total - mt[i, ax, piece(s)]).astype(BF)
            for n in (10, 9, 11):
                sends[n].start()

    def stage_spread(i):
        for ax in (0, 1):
            sends, wait, base, p, pp, pm, s, piece = exch(i, ax)
            wait(9, 10, 11)
            for n in (12, 13, 14, 15):
                sends[n].start()

    def stage_forward(i):
        for ax in (0, 1):
            sends, wait, *_ = exch(i, ax)
            wait(12)
            sends[16].start()
            wait(13)
            sends[17].start()

    def stage_wait(i):
        for ax in (0, 1):
            exch(i, ax)[1](14, 15, 16, 17)

    def back(i, k):
        res = jnp.concatenate([rt[i, q] for q in range(8)], axis=1)
        return masked(jnp.dot(res, u[i, k], preferred_element_type=F32), i, k)

    def stage_back(i):
        stage_wait(i)
        bk = [back(i, k) for k in range(4)]
        for k in range(4):
            for q in range(4):
                rows = slice(256 * q, 256 * q + 256)
                grad[k, :, rows] += lax.dot_general(bk[k], v[i, k, rows], NT, preferred_element_type=F32)

    grad[...] = jnp.zeros_like(grad)

    def slot(t, _):
        def run(lag, last, stage):
            i = t - lag
            pl.when(jnp.logical_and(i >= 0, i < last))(lambda: stage(i))

        run(0, n_i, stage_pred)
        run(LAG_FORWARD, n_i, stage_forward)
        run(LAG_SPREAD, n_i, stage_spread)
        run(LAG_RESID, n_i, stage_resid)
        run(LAG_SUM, n_i, stage_sum)
        run(LAG_RELAY, n_i, stage_relay)
        run(LAG_BACK, n_i - 1, stage_back)
        return 0

    lax.fori_loop(0, n_i + LAG_FORWARD, slot, 0)

    def tail(i, _):
        stage_back(i)
        return 0

    lax.fori_loop(n_i + LAG_FORWARD - LAG_BACK, n_i - 1, tail, 0)

    mine = pl.ds(pl.multiple_of(h * 512, 512), 512)
    other = pl.ds(pl.multiple_of((1 - h) * 512, 512), 512)
    last = n_i - 1
    stage_wait(last)
    core = [Copy((cs, k), (cr, k), (gc_s, k), (gc_r, k), sibling) for k in range(4)]
    for k in (3, 2, 1, 0):
        bk = back(last, k)
        for q in range(4):
            rows = slice(256 * q, 256 * q + 256)
            grad[k, :, rows] += lax.dot_general(bk, v[last, k, rows], NT, preferred_element_type=F32)
        cs[k] = grad[k, :, other].astype(BF)
        core[k].start()

    zsend = [
        Copy((zs, 3, lo), (zd, 0), (gz_s, 0), (gz_r, 0), at_z(zp)),
        Copy((zs, 3, hi), (zd, 1), (gz_s, 1), (gz_r, 1), at_z(zm)),
        Copy((zs, 2, hi), (zr, 0, hi), (gz_s, 2), (gz_r, 2), at_z(zp)),
        Copy((zs, 1, lo), (zr, 1, lo), (gz_s, 3), (gz_r, 3), at_z(zm)),
        Copy((zs, 2, lo), (zr, 0, lo), (gz_s, 4), (gz_r, 4), at_z(zp)),
        Copy((zs, 1, hi), (zr, 1, hi), (gz_s, 5), (gz_r, 5), at_z(zm)),
    ]
    core[3].wait_recv()
    zs[3] = (grad[3, :, mine] + cr[3].astype(F32)).astype(BF)
    zsend[0].start()
    zsend[1].start()
    core[2].wait_recv()
    zs[2, 64:] = (grad[2, 64:, mine] + cr[2, 64:].astype(F32)).astype(BF)
    zsend[2].start()
    core[1].wait_recv()
    zs[1, :64] = (grad[1, :64, mine] + cr[1, :64].astype(F32)).astype(BF)
    zsend[3].start()
    zsend[0].wait_recv()
    zs[2, :64] = (grad[2, :64, mine] + cr[2, :64].astype(F32) + zd[0].astype(F32)).astype(BF)
    zsend[4].start()
    zsend[1].wait_recv()
    zs[1, 64:] = (grad[1, 64:, mine] + cr[1, 64:].astype(F32) + zd[1].astype(F32)).astype(BF)
    zsend[5].start()
    core[0].wait_recv()
    grad[0, :, mine] += cr[0].astype(F32)
    for n in (2, 3, 4, 5):
        zsend[n].wait_recv()
    total = grad[0, :, mine] + zr[0].astype(F32) + zr[1].astype(F32)
    new = (img[...] - total.T).reshape(8, 64, 128)
    moved[...] = new
    m16[...] = new.astype(BF)

    hsend = [
        Copy(m16, (hc, 0), (hs_s, 0), (hs_r, 0), (r, cp)),
        Copy(m16, (hc, 1), (hs_s, 1), (hs_r, 1), (r, cm)),
        Copy((m16, pl.ds(4, 4)), (hr, 0), (hs_s, 2), (hs_r, 2), (rp, c)),
        Copy((m16, pl.ds(0, 4)), (hr, 1), (hs_s, 3), (hs_r, 3), (rm, c)),
        Copy((m16, 7), (hx, 0), (hs_s, 4), (hs_r, 4), (rp, cp)),
        Copy((m16, 6), (hx, 1), (hs_s, 5), (hs_r, 5), (rp, cm)),
        Copy((m16, 1), (hx, 2), (hs_s, 6), (hs_r, 6), (rm, cp)),
        Copy((m16, 0), (hx, 3), (hs_s, 7), (hs_r, 7), (rm, cm)),
    ]
    for n in (4, 5, 6, 7, 0, 1, 2, 3):
        hsend[n].start()

    for cpy in out_x + core + zsend:
        cpy.wait_send()

    def left(i, _):
        for ax in (0, 1):
            for cpy in exch(i, ax)[0]:
                cpy.wait_send()
        return 0

    lax.fori_loop(0, n_i, left, 0)
    for n in range(8):
        hsend[n].wait_recv()

    has = {-1: r > 0, 4: r < 7}
    hasc = {-1: c > 0, 2: c < 15}
    zrow = lax.broadcasted_iota(jnp.int32, (64, 128), 0)

    def inside(a, b):
        conds = []
        if a < 0 or a > 3:
            conds.append(has[-1 if a < 0 else 4])
        if b < 0 or b > 1:
            conds.append(hasc[-1 if b < 0 else 2])
        return conds

    def clip(a, b, value):
        for cond in inside(a, b):
            value = jnp.where(cond, value, 0.0)
        return value

    def first(a, b):
        if 0 <= a <= 3 and 0 <= b <= 1:
            return moved[2 * a + b]
        if 0 <= b <= 1:
            got = hr[0, 2 * (a + 2) + b] if a < 0 else hr[1, 2 * (a - 4) + b]
        elif 0 <= a <= 3:
            got = hc[0, 2 * a + b + 2] if b < 0 else hc[1, 2 * a + b - 2]
        else:
            got = hx[(0 if a < 0 else 2) + (0 if b < 0 else 1)]
        return clip(a, b, got.astype(F32))

    def second(a, b):
        if 0 <= a <= 3 and 0 <= b <= 1:
            return s1[2 * a + b]
        if 0 <= b <= 1:
            return s1[8 + b if a < 0 else 10 + b]
        return s1[12 + a if b < 0 else 16 + a]

    def diffuse(source, cells, store):
        fx, fy = {}, {}

        def edge(table, a, b, da, db):
            if (a, b) not in table:
                table[a, b] = flux(source(a + da, b + db) - source(a, b))
            return table[a, b]

        for a, b in cells:
            center = source(a, b)
            up = jnp.where(zrow == 63, 0.0, pltpu.roll(center, 63, 0))
            fz = flux(up - center)
            edge0 = flux(-center)
            down = jnp.where(zrow == 0, edge0, -pltpu.roll(fz, 1, 0))
            total = edge(fx, a, b, 1, 0) - edge(fx, a - 1, b, 1, 0) + edge(fy, a, b, 0, 1) - edge(fy, a, b - 1, 0, 1)
            total = total + fz + down
            store(a, b, center + 0.12 * total)

    def store1(a, b, value):
        slot_of = 2 * a + b
        if not 0 <= a <= 3:
            slot_of = 8 + b if a < 0 else 10 + b
        elif not 0 <= b <= 1:
            slot_of = 12 + a if b < 0 else 16 + a
        s1[slot_of] = clip(a, b, value)

    def store2(a, b, value):
        out[2 * a + b] = value

    own_cells = [(a, b) for a in range(4) for b in (0, 1)]
    cells1 = [(a, b) for a in range(-1, 5) for b in range(-1, 3) if 0 <= a <= 3 or 0 <= b <= 1]
    diffuse(first, cells1, store1)
    diffuse(second, own_cells, store2)
    for n in range(8):
        hsend[n].wait_send()


def body(image, u_factors, v_factors, ranks, measured):
    row_tiles, col_tiles, tile_len, rank_max = u_factors.shape
    f = image.shape[3]
    voxels = image.shape[0] * image.shape[1] * image.shape[2]
    anywhere = pl.BlockSpec(memory_space=pl.ANY)
    n = row_tiles
    vm = pltpu.VMEM
    dma = pltpu.SemaphoreType.DMA
    new = pl.pallas_call(
        kernel,
        out_shape=jax.ShapeDtypeStruct((8, 64, f), F32),
        in_specs=[anywhere, anywhere, anywhere, pl.BlockSpec(memory_space=pltpu.SMEM), anywhere],
        out_specs=pl.BlockSpec(memory_space=pltpu.VMEM),
        scratch_shapes=[
            vm((voxels, f), F32),
            vm((n, 4, tile_len, rank_max), BF), vm((n, 4, tile_len, rank_max), BF),
            vm((2, n, 128, f), BF), vm((n, 2, f, 128), F32),
            vm((8, f, voxels), BF), vm((n, 4, f, rank_max), BF),
            vm((n, 8, f, 128), BF), vm((n, 2, 2, 64, 128), BF), vm((n, 2, 2, 64, 128), BF),
            vm((n, 2, 2, f, 128), BF), vm((n, 2, f, 128), F32), vm((n, 2, f, 128), BF),
            vm((n, 2, 3, 32, 128), BF), vm((n, 8, f, 128), BF),
            vm((4, f, tile_len), F32), vm((4, f, 512), BF), vm((4, f, 512), BF), vm((4, f, 512), BF),
            vm((2, 64, 512), BF), vm((2, f, 512), BF),
            vm((8, 64, f), F32), vm((8, 64, f), BF), vm((2, 4, 64, f), BF), vm((2, 8, 64, f), BF), vm((4, 64, f), BF),
            vm((20, 64, f), F32),
            dma((11,)), dma((13,)), dma((13,)), dma((n, 2, 18)), dma((n, 2, 18)),
            dma((4,)), dma((4,)), dma((6,)), dma((6,)), dma((8,)), dma((8,)),
        ],
        compiler_params=pltpu.CompilerParams(collective_id=0, has_side_effects=True, vmem_limit_bytes=56 << 20),
        name="step",
    )(
        image.reshape(voxels, f), u_factors, v_factors, ranks.T,
        measured.reshape(n, 2, 4, 128, f),
    )
    return new.reshape(image.shape)


def solution(mesh):
    placed = (
        P("row", "col", None, None),
        P("row", "col", None, None),
        P("row", "col", None, None),
        P("row", "col"),
        P("row", None),
    )
    return jax.shard_map(
        body, mesh=mesh, in_specs=placed, out_specs=P("row", "col", None, None), check_vma=False
    )
```

time: 238 us -> 72.7 us (0.31)
  the two profiles are of different devices: /device:TPU:25 before, /device:TPU:0 now
where the time goes in v1:
time: 72.7 us; the launch traced here: 71.6 us
  Pallas kernels  69.9 us (96%)
  local copies, waits for them, and re-layouts  1.67 us (2%)
    pallas_call x1, Pallas kernels, body(): pl.pallas_call(kernel, out_shape=jax.ShapeDtypeStruct((8, 64, f), F32), i...  69.9 us
    unnamed x1, local copies, waits for them, and re-layouts  1.67 us

profile of v1, /device:TPU:0, one launch (start us, length us, event | category | flops | bytes accessed | tf_op | source)
XLA Modules:
  0.0 71.6 jit_solution(8637580107040537499)
XLA Ops:
  0.0 69.9 %step.1 = f32[8,64,128]{2,1,0:T(8,128)} custom-call(f32[512,128]{1,0:T(8,128)} %bitcast.6, bf16[5,4,1024,256]{3,2,1,0:T(8,128)(2,1)} %u_hbm.1, bf16[5,4,1024,256]{3,2,1,0:T(8,128)(2,1)} %v_hbm.1, s32[4,5]{1,0:T(4,128)} %bitcast.7, bf16[5,2,4,128,128]{4,3,2,1,0:T(8,128)(2,1)} %bitcast.4), custom_call_target="tpu_custom_call" | custom-call | tf_op jit(solution)/shard_map/step/pallas_call | solution.py:477
  69.9 1.7 %copy.7 = f32[4,2,64,128]{3,2,1,0:T(8,128)} copy(f32[4,2,64,128]{3,2,1,0:T(8,128)} %bitcast.5) | data formatting | bytes 524288

commit v2 on v1

--- a/solution.py
+++ b/solution.py
@@ -10,6 +10,8 @@
 BF = jnp.bfloat16
 F32 = jnp.float32
 
+ESEM = (0, 0, 1, 1, 1, 1, 2, 2, 2, 3, 3, 3, 4, 4, 5, 5, 5, 5)
+XSEM = (0, 1, 2, 3, 4, 5, 6, 7, 8, 7, 8, 9, 9)
 LAG_RELAY, LAG_SUM, LAG_RESID, LAG_SPREAD, LAG_FORWARD, LAG_BACK = 2, 4, 6, 8, 10, 12
 
 
@@ -18,9 +20,9 @@
         self.parts = (src, dst, ss, rs, dev)
 
     def made(self):
-        src, dst, (ss, si), (rs, ri), dev = self.parts
+        src, dst, ss, rs, dev = self.parts
         return pltpu.make_async_remote_copy(
-            src_ref=at(src), dst_ref=at(dst), send_sem=ss.at[si], recv_sem=rs.at[ri], device_id=dev, device_id_type=MESH)
+            src_ref=at(src), dst_ref=at(dst), send_sem=at(ss), recv_sem=at(rs), device_id=dev, device_id_type=MESH)
 
     def start(self):
         self.made().start()
@@ -28,8 +30,10 @@
     def wait_recv(self):
         self.made().wait_recv()
 
-    def wait_send(self):
-        self.made().wait_send()
+
+def arrived(like, sem):
+    ref = at(like)
+    pltpu.make_async_copy(ref, ref, at(sem)).wait()
 
 
 def at(place):
@@ -44,8 +48,8 @@
 
 
 def kernel(
-    img_hbm, u_hbm, v_hbm, ranks, meas_hbm, out,
-    img, u, v, mb, mt, xt, coef,
+    img_hbm, u_hbm, v_hbm, ranks_hbm, meas_hbm, out,
+    ranks, img, u, v, mb, mt, xt, coef,
     ps, d2, qb, r1, sums, ph2, r2, rt,
     grad, cs, cr, zs, zd, zr, moved, m16, hr, hc, hx, s1,
     lsem, ax_s, ax_r, ex_s, ex_r, gc_s, gc_r, gz_s, gz_r, hs_s, hs_r,
@@ -60,10 +64,12 @@
 
     img_copy = pltpu.make_async_copy(img_hbm, img, lsem.at[0])
     img_copy.start()
+    r_copy = pltpu.make_async_copy(ranks_hbm, ranks, lsem.at[7])
+    r_copy.start()
     v_copies = [pltpu.make_async_copy(v_hbm.at[:, order[k]], v.at[:, k], lsem.at[1 + k]) for k in range(4)]
-    u_copies = [pltpu.make_async_copy(u_hbm.at[:, order[k]], u.at[:, k], lsem.at[5 + k]) for k in range(4)]
-    m_copies = [pltpu.make_async_copy(meas_hbm.at[:, 0, x], mb.at[0], lsem.at[9]),
-                pltpu.make_async_copy(meas_hbm.at[:, 1, y], mb.at[1], lsem.at[10])]
+    u_copies = [pltpu.make_async_copy(u_hbm.at[:, order[k]], u.at[:, k], lsem.at[5]) for k in range(4)]
+    m_copies = [pltpu.make_async_copy(meas_hbm.at[:, 0, x], mb.at[0], lsem.at[6]),
+                pltpu.make_async_copy(meas_hbm.at[:, 1, y], mb.at[1], lsem.at[6])]
 
     def at_z(zz, hh=h):
         return (zz * 2 + hh, c)
@@ -100,7 +106,7 @@
 
     def xcopy(i, blk, part, dev):
         ref = (xt, blk) if part is None else (xt, blk, part)
-        return Copy(ref, ref, (ax_s, i), (ax_r, i), dev)
+        return Copy(ref, ref, (ax_s, 1 if i in (1, 2) else 0), (ax_r, XSEM[i]), dev)
 
     b0, bm, bp, bf = r, zm * 2 + h, zp * 2 + h, zf * 2 + h
     o0, om, op, of = z * 2 + 1 - h, zm * 2 + 1 - h, zp * 2 + 1 - h, zf * 2 + 1 - h
@@ -111,15 +117,14 @@
         xcopy(7, bm, lo, sibling), xcopy(8, bp, hi, sibling), xcopy(9, bm, hi, sibling), xcopy(10, bp, lo, sibling),
         xcopy(11, bf, lo, sibling), xcopy(12, bf, hi, sibling),
     ]
-    in_x = [
-        xcopy(0, o0, None, sibling),
-        xcopy(1, bm, lo, sibling), xcopy(2, bp, hi, sibling), xcopy(3, bm, hi, sibling), xcopy(4, bp, lo, sibling),
-        xcopy(5, bf, lo, sibling), xcopy(6, bf, hi, sibling),
-        xcopy(7, om, lo, sibling), xcopy(8, op, hi, sibling), xcopy(9, om, hi, sibling), xcopy(10, op, lo, sibling),
-        xcopy(11, of, lo, sibling), xcopy(12, of, hi, sibling),
-    ]
-    for i in (1, 2, 0, 3, 4):
+    half = (xt, 0, lo)
+    whole = (xt, 0)
+    for i in (1, 2, 0):
         out_x[i].start()
+    arrived(whole, (ax_s, 1))
+    for i in (3, 4):
+        out_x[i].start()
+    r_copy.wait()
 
     lane = lax.broadcasted_iota(jnp.int32, (128, 256), 1)
 
@@ -137,16 +142,15 @@
 
         lax.fori_loop(0, n_i, one, 0)
 
-    in_x[0].wait_recv()
+    arrived(whole, (ax_r, 0))
     coefs(0)
-    in_x[1].wait_recv()
+    arrived(half, (ax_r, 1))
     out_x[5].start()
     out_x[7].start()
-    in_x[2].wait_recv()
+    arrived(half, (ax_r, 2))
     out_x[6].start()
     out_x[8].start()
-    for m in m_copies:
-        m.wait()
+    arrived(mb, (lsem, 6))
 
     def turn(i, _):
         for ax in (0, 1):
@@ -154,25 +158,21 @@
         return 0
 
     lax.fori_loop(0, n_i, turn, 0)
-    in_x[3].wait_recv()
+    arrived(half, (ax_r, 3))
     out_x[9].start()
-    in_x[4].wait_recv()
+    arrived(half, (ax_r, 4))
     out_x[10].start()
-    in_x[7].wait_recv()
-    in_x[9].wait_recv()
+    arrived(whole, (ax_r, 7))
     coefs(1)
-    in_x[8].wait_recv()
-    in_x[10].wait_recv()
+    arrived(whole, (ax_r, 8))
     coefs(2)
-    in_x[5].wait_recv()
+    arrived(half, (ax_r, 5))
     out_x[11].start()
-    in_x[6].wait_recv()
+    arrived(half, (ax_r, 6))
     out_x[12].start()
-    in_x[11].wait_recv()
-    in_x[12].wait_recv()
+    arrived(whole, (ax_r, 9))
     coefs(3)
-    for k in range(4):
-        u_copies[k].wait()
+    arrived(u, (lsem, 5))
 
     axes = (
         (0, x, along_x, y, along_y),
@@ -184,7 +184,7 @@
         pp, pm, pf = (p + 1) % 4, (p + 3) % 4, (p + 2) % 4
 
         def cpy(n, src, dst, dev):
-            return Copy(src, dst, (ex_s, (i, ax, n)), (ex_r, (i, ax, n)), dev)
+            return Copy(src, dst, (ex_s, i), (ex_r, i, ESEM[n]), dev)
 
         def piece(pos):
             return pl.ds(pl.multiple_of(pos * 32, 32), 32)
@@ -210,17 +210,7 @@
             cpy(16, (rt, i, base + pm, lo), (rt, i, base + pm, lo), dev1(pp)),
             cpy(17, (rt, i, base + pp, hi), (rt, i, base + pp, hi), dev1(pm)),
         ]
-        lands = [(d2, i, ax, 0), (d2, i, ax, 1), (r1, i, ax, 0, hi), (r1, i, ax, 1, lo), (r1, i, ax, 0, lo), (r1, i, ax, 1, hi)]
-        lands += [(r2, i, ax, d - 1) for d in (1, 2, 3)]
-        lands += [own + (piece((s + 4 - d) % 4),) for d in (1, 2, 3)]
-        lands += [(rt, i, base + pm, lo), (rt, i, base + pp, hi), (rt, i, base + pm, hi), (rt, i, base + pp, lo),
-                  (rt, i, base + pf, lo), (rt, i, base + pf, hi)]
-
-        def wait(*ns):
-            for n in ns:
-                cpy(n, lands[n], lands[n], dev1(pp)).wait_recv()
-
-        return sends, wait, base, p, pp, pm, s, piece
+        return sends, base, p, pp, pm, s, piece
 
     def stage_pred(i):
         cf = [coef[i, k] for k in range(4)]
@@ -237,19 +227,18 @@
                 sends[n].start()
 
     def stage_relay(i):
-        for ax in (0, 1):
-            sends, wait, base, p, pp, pm, s, piece = exch(i, ax)
-            wait(0)
+        arrived((d2, i), (ex_r, i, 0))
+        for ax in (0, 1):
+            sends, base, p, pp, pm, s, piece = exch(i, ax)
             qb[i, ax, 0] = (ps[i, base + pp, :64].astype(F32) + d2[i, ax, 0].astype(F32)).astype(BF)
             sends[4].start()
-            wait(1)
             qb[i, ax, 1] = (ps[i, base + pm, 64:].astype(F32) + d2[i, ax, 1].astype(F32)).astype(BF)
             sends[5].start()
 
     def stage_sum(i):
-        for ax in (0, 1):
-            sends, wait, base, p, pp, pm, s, piece = exch(i, ax)
-            wait(2, 3, 4, 5)
+        arrived((r1, i), (ex_r, i, 1))
+        for ax in (0, 1):
+            sends, base, p, pp, pm, s, piece = exch(i, ax)
             total = ps[i, base + p].astype(F32) + r1[i, ax, 0].astype(F32) + r1[i, ax, 1].astype(F32)
             sums[i, ax] = total
             ph2[i, ax] = total.astype(BF)
@@ -257,9 +246,9 @@
                 sends[n].start()
 
     def stage_resid(i):
-        for ax in (0, 1):
-            sends, wait, base, p, pp, pm, s, piece = exch(i, ax)
-            wait(6, 7, 8)
+        arrived((r2, i), (ex_r, i, 2))
+        for ax in (0, 1):
+            sends, base, p, pp, pm, s, piece = exch(i, ax)
             total = sums[i, ax, piece(s)]
             for d in range(3):
                 total += r2[i, ax, d].astype(F32)
@@ -268,23 +257,21 @@
                 sends[n].start()
 
     def stage_spread(i):
-        for ax in (0, 1):
-            sends, wait, base, p, pp, pm, s, piece = exch(i, ax)
-            wait(9, 10, 11)
+        arrived((r2, i), (ex_r, i, 3))
+        for ax in (0, 1):
+            sends, base, p, pp, pm, s, piece = exch(i, ax)
             for n in (12, 13, 14, 15):
                 sends[n].start()
 
     def stage_forward(i):
-        for ax in (0, 1):
-            sends, wait, *_ = exch(i, ax)
-            wait(12)
+        arrived((d2, i), (ex_r, i, 4))
+        for ax in (0, 1):
+            sends = exch(i, ax)[0]
             sends[16].start()
-            wait(13)
             sends[17].start()
 
     def stage_wait(i):
-        for ax in (0, 1):
-            exch(i, ax)[1](14, 15, 16, 17)
+        arrived((r1, i), (ex_r, i, 5))
 
     def back(i, k):
         res = jnp.concatenate([rt[i, q] for q in range(8)], axis=1)
@@ -326,7 +313,7 @@
     other = pl.ds(pl.multiple_of((1 - h) * 512, 512), 512)
     last = n_i - 1
     stage_wait(last)
-    core = [Copy((cs, k), (cr, k), (gc_s, k), (gc_r, k), sibling) for k in range(4)]
+    core = [Copy((cs, k), (cr, k), (gc_s, 0), (gc_r, k), sibling) for k in range(4)]
     for k in (3, 2, 1, 0):
         bk = back(last, k)
         for q in range(4):
@@ -337,11 +324,11 @@
 
     zsend = [
         Copy((zs, 3, lo), (zd, 0), (gz_s, 0), (gz_r, 0), at_z(zp)),
-        Copy((zs, 3, hi), (zd, 1), (gz_s, 1), (gz_r, 1), at_z(zm)),
-        Copy((zs, 2, hi), (zr, 0, hi), (gz_s, 2), (gz_r, 2), at_z(zp)),
-        Copy((zs, 1, lo), (zr, 1, lo), (gz_s, 3), (gz_r, 3), at_z(zm)),
-        Copy((zs, 2, lo), (zr, 0, lo), (gz_s, 4), (gz_r, 4), at_z(zp)),
-        Copy((zs, 1, hi), (zr, 1, hi), (gz_s, 5), (gz_r, 5), at_z(zm)),
+        Copy((zs, 3, hi), (zd, 1), (gz_s, 0), (gz_r, 1), at_z(zm)),
+        Copy((zs, 2, hi), (zr, 0, hi), (gz_s, 0), (gz_r, 2), at_z(zp)),
+        Copy((zs, 1, lo), (zr, 1, lo), (gz_s, 0), (gz_r, 2), at_z(zm)),
+        Copy((zs, 2, lo), (zr, 0, lo), (gz_s, 0), (gz_r, 2), at_z(zp)),
+        Copy((zs, 1, hi), (zr, 1, hi), (gz_s, 0), (gz_r, 2), at_z(zm)),
     ]
     core[3].wait_recv()
     zs[3] = (grad[3, :, mine] + cr[3].astype(F32)).astype(BF)
@@ -361,8 +348,7 @@
     zsend[5].start()
     core[0].wait_recv()
     grad[0, :, mine] += cr[0].astype(F32)
-    for n in (2, 3, 4, 5):
-        zsend[n].wait_recv()
+    arrived(zr, (gz_r, 2))
     total = grad[0, :, mine] + zr[0].astype(F32) + zr[1].astype(F32)
     new = (img[...] - total.T).reshape(8, 64, 128)
     moved[...] = new
@@ -370,29 +356,23 @@
 
     hsend = [
         Copy(m16, (hc, 0), (hs_s, 0), (hs_r, 0), (r, cp)),
-        Copy(m16, (hc, 1), (hs_s, 1), (hs_r, 1), (r, cm)),
-        Copy((m16, pl.ds(4, 4)), (hr, 0), (hs_s, 2), (hs_r, 2), (rp, c)),
-        Copy((m16, pl.ds(0, 4)), (hr, 1), (hs_s, 3), (hs_r, 3), (rm, c)),
-        Copy((m16, 7), (hx, 0), (hs_s, 4), (hs_r, 4), (rp, cp)),
-        Copy((m16, 6), (hx, 1), (hs_s, 5), (hs_r, 5), (rp, cm)),
-        Copy((m16, 1), (hx, 2), (hs_s, 6), (hs_r, 6), (rm, cp)),
-        Copy((m16, 0), (hx, 3), (hs_s, 7), (hs_r, 7), (rm, cm)),
+        Copy(m16, (hc, 1), (hs_s, 0), (hs_r, 0), (r, cm)),
+        Copy((m16, pl.ds(4, 4)), (hr, 0), (hs_s, 0), (hs_r, 0), (rp, c)),
+        Copy((m16, pl.ds(0, 4)), (hr, 1), (hs_s, 0), (hs_r, 0), (rm, c)),
+        Copy((m16, 7), (hx, 0), (hs_s, 0), (hs_r, 0), (rp, cp)),
+        Copy((m16, 6), (hx, 1), (hs_s, 0), (hs_r, 0), (rp, cm)),
+        Copy((m16, 1), (hx, 2), (hs_s, 0), (hs_r, 0), (rm, cp)),
+        Copy((m16, 0), (hx, 3), (hs_s, 0), (hs_r, 0), (rm, cm)),
     ]
     for n in (4, 5, 6, 7, 0, 1, 2, 3):
         hsend[n].start()
 
-    for cpy in out_x + core + zsend:
-        cpy.wait_send()
-
-    def left(i, _):
-        for ax in (0, 1):
-            for cpy in exch(i, ax)[0]:
-                cpy.wait_send()
-        return 0
-
-    lax.fori_loop(0, n_i, left, 0)
-    for n in range(8):
-        hsend[n].wait_recv()
+    arrived((xt, pl.ds(0, 6)), (ax_s, 0))
+    arrived(cs, (gc_s, 0))
+    arrived((zs, pl.ds(0, 3)), (gz_s, 0))
+    for i in range(n_i):
+        arrived((v, 0, 0, pl.ds(0, 960)), (ex_s, i))
+    arrived((v, 0, 0, pl.ds(0, 896)), (hs_r, 0))
 
     has = {-1: r > 0, 4: r < 7}
     hasc = {-1: c > 0, 2: c < 15}
@@ -462,8 +442,7 @@
     cells1 = [(a, b) for a in range(-1, 5) for b in range(-1, 3) if 0 <= a <= 3 or 0 <= b <= 1]
     diffuse(first, cells1, store1)
     diffuse(second, own_cells, store2)
-    for n in range(8):
-        hsend[n].wait_send()
+    arrived((v, 0, 0, pl.ds(0, 896)), (hs_s, 0))
 
 
 def body(image, u_factors, v_factors, ranks, measured):
@@ -476,11 +455,11 @@
     dma = pltpu.SemaphoreType.DMA
     new = pl.pallas_call(
         kernel,
-        out_shape=jax.ShapeDtypeStruct((8, 64, f), F32),
-        in_specs=[anywhere, anywhere, anywhere, pl.BlockSpec(memory_space=pltpu.SMEM), anywhere],
+        out_shape=pltpu.VMEM((8, 64, f), F32),
+        in_specs=[anywhere] * 5,
         out_specs=pl.BlockSpec(memory_space=pltpu.VMEM),
         scratch_shapes=[
-            vm((voxels, f), F32),
+            pltpu.SMEM((4, n), jnp.int32), vm((voxels, f), F32),
             vm((n, 4, tile_len, rank_max), BF), vm((n, 4, tile_len, rank_max), BF),
             vm((2, n, 128, f), BF), vm((n, 2, f, 128), F32),
             vm((8, f, voxels), BF), vm((n, 4, f, rank_max), BF),
@@ -491,8 +470,8 @@
             vm((2, 64, 512), BF), vm((2, f, 512), BF),
             vm((8, 64, f), F32), vm((8, 64, f), BF), vm((2, 4, 64, f), BF), vm((2, 8, 64, f), BF), vm((4, 64, f), BF),
             vm((20, 64, f), F32),
-            dma((11,)), dma((13,)), dma((13,)), dma((n, 2, 18)), dma((n, 2, 18)),
-            dma((4,)), dma((4,)), dma((6,)), dma((6,)), dma((8,)), dma((8,)),
+            dma((8,)), dma((2,)), dma((10,)), dma((n,)), dma((n, 6)),
+            dma((1,)), dma((4,)), dma((1,)), dma((3,)), dma((1,)), dma((1,)),
         ],
         compiler_params=pltpu.CompilerParams(collective_id=0, has_side_effects=True, vmem_limit_bytes=56 << 20),
         name="step",

time: 72.7 us -> 67.2 us (0.924)
  Pallas kernels: 69.9 us -> 65.7 us
  local copies, waits for them, and re-layouts: 1.67 us -> 0.71 us
    pallas_call x1, Pallas kernels: 69.9 us -> 65.7 us  [body(): pl.pallas_call(kernel, out_shape=pltpu.VMEM((8, 64, f), F32), in_specs=[a...]
    unnamed x1, local copies, waits for them, and re-layouts: 1.67 us -> 0.71 us
where the time goes in v2:
time: 67.2 us; the launch traced here: 66.4 us
  Pallas kernels  65.7 us (98%)
  local copies, waits for them, and re-layouts  0.71 us (1%)
    pallas_call x1, Pallas kernels, body(): pl.pallas_call(kernel, out_shape=pltpu.VMEM((8, 64, f), F32), in_specs=[a...  65.7 us

profile of v2, /device:TPU:0, one launch (start us, length us, event | category | flops | bytes accessed | tf_op | source)
XLA Modules:
  0.0 66.4 jit_solution(10413980162212673807)
XLA Ops:
  0.0 65.7 %step.1 = f32[8,64,128]{2,1,0:T(8,128)S(1)} custom-call(f32[512,128]{1,0:T(8,128)} %bitcast.6, bf16[5,4,1024,256]{3,2,1,0:T(8,128)(2,1)} %u_hbm.1, bf16[5,4,1024,256]{3,2,1,0:T(8,128)(2,1)} %v_hbm.1, s32[4,5]{1,0:T(4,128)} %bitcast.7, bf16[5,2,4,128,128]{4,3,2,1,0:T(8,128)(2,1)} %bitcast.5), custom_call_target="tpu_custom_call" | custom-call | tf_op jit(solution)/shard_map/step/pallas_call | solution.py:456
  65.7 0.7 %copy.7 = f32[4,2,64,128]{3,2,1,0:T(8,128)} copy(f32[4,2,64,128]{3,2,1,0:T(8,128)S(1)} %bitcast.4) | data formatting | bytes 524288

commit v3 on v2

--- a/solution.py
+++ b/solution.py
@@ -10,9 +10,8 @@
 BF = jnp.bfloat16
 F32 = jnp.float32
 
-ESEM = (0, 0, 1, 1, 1, 1, 2, 2, 2, 3, 3, 3, 4, 4, 5, 5, 5, 5)
 XSEM = (0, 1, 2, 3, 4, 5, 6, 7, 8, 7, 8, 9, 9)
-LAG_RELAY, LAG_SUM, LAG_RESID, LAG_SPREAD, LAG_FORWARD, LAG_BACK = 2, 4, 6, 8, 10, 12
+GROUPS = tuple((i, 1) for i in range(5))
 
 
 class Copy:
@@ -50,9 +49,9 @@
 def kernel(
     img_hbm, u_hbm, v_hbm, ranks_hbm, meas_hbm, out,
     ranks, img, u, v, mb, mt, xt, coef,
-    ps, d2, qb, r1, sums, ph2, r2, rt,
+    ps, kept, r1, sums, ph2, r2, rt,
     grad, cs, cr, zs, zd, zr, moved, m16, hr, hc, hx, s1,
-    lsem, ax_s, ax_r, ex_s, ex_r, gc_s, gc_r, gz_s, gz_r, hs_s, hs_r,
+    lsem, ax_s, ax_r, ex_s, ex_r, gc_s, gc_r, gz_s, gz_r, hs_s, hs_r, ready,
 ):
     n_i = u.shape[0]
     r = lax.axis_index("row")
@@ -84,9 +83,8 @@
     def along_y(pos):
         return (r, pos * 4 + x)
 
-    peers = [sibling, at_z(zp), at_z(zm)]
-    peers += [along_x((x + d) % 4) for d in (1, 2, 3)] + [along_y((y + d) % 4) for d in (1, 2, 3)]
-    peers += [(rp, c), (rm, c), (r, cp), (r, cm), (rp, cp), (rp, cm), (rm, cp), (rm, cm)]
+    sides = [along_x((x + 1) % 4), along_x((x + 3) % 4), along_y((y + 1) % 4), along_y((y + 3) % 4)]
+    peers = [sibling, at_z(zp), at_z(zm)] + sides
     barrier = pltpu.get_barrier_semaphore()
     for peer in peers:
         pl.semaphore_signal(barrier, inc=1, device_id=peer, device_id_type=MESH)
@@ -101,6 +99,8 @@
         u_copies[k].start()
     xt[r] = img[...].T.astype(BF)
     pl.semaphore_wait(barrier, len(peers))
+    for peer in sides:
+        pl.semaphore_signal(ready, inc=1, device_id=peer, device_id_type=MESH)
 
     lo, hi = pl.ds(0, 64), pl.ds(64, 64)
 
@@ -131,13 +131,16 @@
     def masked(value, i, k):
         return jnp.where(lane < ranks[order[k], i], value, 0.0).astype(BF)
 
+    def coef_of(i, k):
+        j = order[k]
+        xj = jnp.concatenate([xt[2 * j], xt[2 * j + 1]], axis=1)
+        return masked(jnp.dot(xj, v[i, k], preferred_element_type=F32), i, k)
+
     def coefs(k):
         v_copies[k].wait()
 
         def one(i, _):
-            j = order[k]
-            xj = jnp.concatenate([xt[2 * j], xt[2 * j + 1]], axis=1)
-            coef[i, k] = masked(jnp.dot(xj, v[i, k], preferred_element_type=F32), i, k)
+            coef[i, k] = coef_of(i, k)
             return 0
 
         lax.fori_loop(0, n_i, one, 0)
@@ -164,161 +167,126 @@
     out_x[10].start()
     arrived(whole, (ax_r, 7))
     coefs(1)
-    arrived(whole, (ax_r, 8))
-    coefs(2)
     arrived(half, (ax_r, 5))
     out_x[11].start()
     arrived(half, (ax_r, 6))
     out_x[12].start()
+    arrived(whole, (ax_r, 8))
+    coefs(2)
+    v_copies[3].wait()
+    arrived(u, (lsem, 5))
+    pl.semaphore_wait(ready, len(sides))
     arrived(whole, (ax_r, 9))
-    coefs(3)
-    arrived(u, (lsem, 5))
-
-    axes = (
-        (0, x, along_x, y, along_y),
-        (4, y, along_y, x, along_x),
-    )
-
-    def exch(i, ax):
-        base, p, dev1, s, dev2 = axes[ax]
-        pp, pm, pf = (p + 1) % 4, (p + 3) % 4, (p + 2) % 4
-
-        def cpy(n, src, dst, dev):
-            return Copy(src, dst, (ex_s, i), (ex_r, i, ESEM[n]), dev)
-
-        def piece(pos):
-            return pl.ds(pl.multiple_of(pos * 32, 32), 32)
-
-        own = (rt, i, base + p)
-        sends = [
-            cpy(0, (ps, i, base + pf, lo), (d2, i, ax, 0), dev1(pp)),
-            cpy(1, (ps, i, base + pf, hi), (d2, i, ax, 1), dev1(pm)),
-            cpy(2, (ps, i, base + pp, hi), (r1, i, ax, 0, hi), dev1(pp)),
-            cpy(3, (ps, i, base + pm, lo), (r1, i, ax, 1, lo), dev1(pm)),
-            cpy(4, (qb, i, ax, 0), (r1, i, ax, 0, lo), dev1(pp)),
-            cpy(5, (qb, i, ax, 1), (r1, i, ax, 1, hi), dev1(pm)),
-        ]
-        for d in (1, 2, 3):
-            sends.append(cpy(5 + d, (ph2, i, ax, piece((s + d) % 4)), (r2, i, ax, d - 1), dev2((s + d) % 4)))
-        for d in (1, 2, 3):
-            sends.append(cpy(8 + d, own + (piece(s),), own + (piece(s),), dev2((s + d) % 4)))
-        sends += [
-            cpy(12, own + (lo,), own + (lo,), dev1(pp)),
-            cpy(13, own + (hi,), own + (hi,), dev1(pm)),
-            cpy(14, own + (hi,), own + (hi,), dev1(pp)),
-            cpy(15, own + (lo,), own + (lo,), dev1(pm)),
-            cpy(16, (rt, i, base + pm, lo), (rt, i, base + pm, lo), dev1(pp)),
-            cpy(17, (rt, i, base + pp, hi), (rt, i, base + pp, hi), dev1(pm)),
-        ]
-        return sends, base, p, pp, pm, s, piece
-
-    def stage_pred(i):
-        cf = [coef[i, k] for k in range(4)]
+
+    axes = ((x, along_x, y, along_y), (y, along_y, x, along_x))
+
+    def send(g, n, src, dst, dev):
+        Copy(src, dst, (ex_s, g), (ex_r, g, n), dev).start()
+
+    def product(g):
+        first, count = GROUPS[g]
+
+        i = first
+        cf = [coef[i, k] for k in range(3)] + [coef_of(i, 3)]
+        tiles = pl.ds(first, count)
+        for ax in (0, 1):
+            p, dev1, s, dev2 = axes[ax]
+            for q in (2 * ax, 2 * ax + 1):
+                rows = slice(256 * q, 256 * q + 256)
+                total = lax.dot_general(cf[0], u[i, 0, rows], NT, preferred_element_type=F32)
+                for k in (1, 2, 3):
+                    total += lax.dot_general(cf[k], u[i, k, rows], NT, preferred_element_type=F32)
+                for e in (0, 1):
+                    role = ((2 * q + e) % 4 - p + 4) % 4
+                    part = total[:, 128 * e:128 * e + 128]
+                    kept[ax, role, i] = part
+                    ps[ax, role, i] = part.astype(BF)
+            for d in (2, 1, 3):
+                send(g, 0, (ps, ax, d, tiles), (r1, ax, d - 1, tiles), dev1((p + d) % 4))
+
+    def total_of(g):
+        first, count = GROUPS[g]
+        tiles = pl.ds(first, count)
+        every = slice(None)
+        arrived((r1, every, every, tiles), (ex_r, g, 0))
+        for ax in (0, 1):
+            p, dev1, s, dev2 = axes[ax]
+            for i in range(first, first + count):
+                part = kept[ax, 0, i]
+                for d in range(3):
+                    part += r1[ax, d, i].astype(F32)
+                for piece in range(4):
+                    role = (piece - s + 4) % 4
+                    sums[ax, role, i] = part[32 * piece:32 * piece + 32]
+                    ph2[ax, role, i] = part[32 * piece:32 * piece + 32].astype(BF)
+            for d in (2, 1, 3):
+                send(g, 1, (ph2, ax, d, tiles), (r2, ax, d - 1, tiles), dev2((s + d) % 4))
+
+    def resid(g):
+        first, count = GROUPS[g]
+        tiles = pl.ds(first, count)
+        every = slice(None)
+        arrived((r2, every, every, tiles), (ex_r, g, 1))
+        for ax in (0, 1):
+            p, dev1, s, dev2 = axes[ax]
+            for i in range(first, first + count):
+                part = sums[ax, 0, i]
+                for d in range(3):
+                    part += r2[ax, d, i].astype(F32)
+                rt[ax, p, s, i] = (part - mt[i, ax, pl.ds(pl.multiple_of(s * 32, 32), 32)]).astype(BF)
+            mine = (rt, ax, p, s, tiles)
+            for d in (2, 1, 3):
+                send(g, 2, mine, mine, dev2((s + d) % 4))
+
+    def spread(g):
+        first, count = GROUPS[g]
+        tiles = pl.ds(first, count)
+        every = slice(None)
+        arrived((r2, every, every, tiles), (ex_r, g, 2))
+        for d in (2, 1, 3):
+            for ax in (0, 1):
+                p, dev1, s, dev2 = axes[ax]
+                mine = (rt, ax, p, slice(None), tiles)
+                send(g, 3, mine, mine, dev1((p + d) % 4))
+
+    def landed(g):
+        first, count = GROUPS[g]
+        every = slice(None)
+        arrived((r1, every, every, pl.ds(first, count)), (ex_r, g, 3))
+
+    def back(i, k):
+        res = jnp.concatenate([rt[q // 4, q % 4, :, i].reshape(128, 128) for q in range(8)], axis=1)
+        return masked(jnp.dot(res, u[i, k], preferred_element_type=F32), i, k)
+
+    def adjoint(g, k):
+        first, count = GROUPS[g]
+        bk = [back(i, k) for i in range(first, first + count)]
         for q in range(4):
             rows = slice(256 * q, 256 * q + 256)
-            total = lax.dot_general(cf[0], u[i, 0, rows], NT, preferred_element_type=F32)
-            for k in (1, 2, 3):
-                total += lax.dot_general(cf[k], u[i, k, rows], NT, preferred_element_type=F32)
-            ps[i, 2 * q] = total[:, :128].astype(BF)
-            ps[i, 2 * q + 1] = total[:, 128:].astype(BF)
-        both = [exch(i, ax)[0] for ax in (0, 1)]
-        for n in range(4):
-            for sends in both:
-                sends[n].start()
-
-    def stage_relay(i):
-        arrived((d2, i), (ex_r, i, 0))
-        for ax in (0, 1):
-            sends, base, p, pp, pm, s, piece = exch(i, ax)
-            qb[i, ax, 0] = (ps[i, base + pp, :64].astype(F32) + d2[i, ax, 0].astype(F32)).astype(BF)
-            sends[4].start()
-            qb[i, ax, 1] = (ps[i, base + pm, 64:].astype(F32) + d2[i, ax, 1].astype(F32)).astype(BF)
-            sends[5].start()
-
-    def stage_sum(i):
-        arrived((r1, i), (ex_r, i, 1))
-        for ax in (0, 1):
-            sends, base, p, pp, pm, s, piece = exch(i, ax)
-            total = ps[i, base + p].astype(F32) + r1[i, ax, 0].astype(F32) + r1[i, ax, 1].astype(F32)
-            sums[i, ax] = total
-            ph2[i, ax] = total.astype(BF)
-            for n in (7, 6, 8):
-                sends[n].start()
-
-    def stage_resid(i):
-        arrived((r2, i), (ex_r, i, 2))
-        for ax in (0, 1):
-            sends, base, p, pp, pm, s, piece = exch(i, ax)
-            total = sums[i, ax, piece(s)]
-            for d in range(3):
-                total += r2[i, ax, d].astype(F32)
-            rt[i, base + p, piece(s)] = (total - mt[i, ax, piece(s)]).astype(BF)
-            for n in (10, 9, 11):
-                sends[n].start()
-
-    def stage_spread(i):
-        arrived((r2, i), (ex_r, i, 3))
-        for ax in (0, 1):
-            sends, base, p, pp, pm, s, piece = exch(i, ax)
-            for n in (12, 13, 14, 15):
-                sends[n].start()
-
-    def stage_forward(i):
-        arrived((d2, i), (ex_r, i, 4))
-        for ax in (0, 1):
-            sends = exch(i, ax)[0]
-            sends[16].start()
-            sends[17].start()
-
-    def stage_wait(i):
-        arrived((r1, i), (ex_r, i, 5))
-
-    def back(i, k):
-        res = jnp.concatenate([rt[i, q] for q in range(8)], axis=1)
-        return masked(jnp.dot(res, u[i, k], preferred_element_type=F32), i, k)
-
-    def stage_back(i):
-        stage_wait(i)
-        bk = [back(i, k) for k in range(4)]
+            total = grad[k, :, rows] if g else None
+            for i, b in zip(range(first, first + count), bk):
+                term = lax.dot_general(b, v[i, k, rows], NT, preferred_element_type=F32)
+                total = term if total is None else total + term
+            grad[k, :, rows] = total
+
+    def adjoints(g):
+        landed(g)
         for k in range(4):
-            for q in range(4):
-                rows = slice(256 * q, 256 * q + 256)
-                grad[k, :, rows] += lax.dot_general(bk[k], v[i, k, rows], NT, preferred_element_type=F32)
-
-    grad[...] = jnp.zeros_like(grad)
-
-    def slot(t, _):
-        def run(lag, last, stage):
-            i = t - lag
-            pl.when(jnp.logical_and(i >= 0, i < last))(lambda: stage(i))
-
-        run(0, n_i, stage_pred)
-        run(LAG_FORWARD, n_i, stage_forward)
-        run(LAG_SPREAD, n_i, stage_spread)
-        run(LAG_RESID, n_i, stage_resid)
-        run(LAG_SUM, n_i, stage_sum)
-        run(LAG_RELAY, n_i, stage_relay)
-        run(LAG_BACK, n_i - 1, stage_back)
-        return 0
-
-    lax.fori_loop(0, n_i + LAG_FORWARD, slot, 0)
-
-    def tail(i, _):
-        stage_back(i)
-        return 0
-
-    lax.fori_loop(n_i + LAG_FORWARD - LAG_BACK, n_i - 1, tail, 0)
+            adjoint(g, k)
+
+    p, t, d, a, b = product, total_of, resid, spread, adjoints
+    for stage, g in (
+        (p, 0), (p, 1), (p, 2), (p, 3), (t, 0), (p, 4), (t, 1), (t, 2), (d, 0), (t, 3), (d, 1), (t, 4), (d, 2), (a, 0), (d, 3), (a, 1), (d, 4), (a, 2), (b, 0), (a, 3), (a, 4), (b, 1), (b, 2), (b, 3),
+    ):
+        stage(g)
 
     mine = pl.ds(pl.multiple_of(h * 512, 512), 512)
     other = pl.ds(pl.multiple_of((1 - h) * 512, 512), 512)
-    last = n_i - 1
-    stage_wait(last)
+    final = len(GROUPS) - 1
+    landed(final)
     core = [Copy((cs, k), (cr, k), (gc_s, 0), (gc_r, k), sibling) for k in range(4)]
     for k in (3, 2, 1, 0):
-        bk = back(last, k)
-        for q in range(4):
-            rows = slice(256 * q, 256 * q + 256)
-            grad[k, :, rows] += lax.dot_general(bk, v[last, k, rows], NT, preferred_element_type=F32)
+        adjoint(final, k)
         cs[k] = grad[k, :, other].astype(BF)
         core[k].start()
 
@@ -370,8 +338,8 @@
     arrived((xt, pl.ds(0, 6)), (ax_s, 0))
     arrived(cs, (gc_s, 0))
     arrived((zs, pl.ds(0, 3)), (gz_s, 0))
-    for i in range(n_i):
-        arrived((v, 0, 0, pl.ds(0, 960)), (ex_s, i))
+    for g, (first, count) in enumerate(GROUPS):
+        arrived((v, pl.ds(0, count), 0, pl.ds(0, 960)), (ex_s, g))
     arrived((v, 0, 0, pl.ds(0, 896)), (hs_r, 0))
 
     has = {-1: r > 0, 4: r < 7}
@@ -462,16 +430,15 @@
             pltpu.SMEM((4, n), jnp.int32), vm((voxels, f), F32),
             vm((n, 4, tile_len, rank_max), BF), vm((n, 4, tile_len, rank_max), BF),
             vm((2, n, 128, f), BF), vm((n, 2, f, 128), F32),
-            vm((8, f, voxels), BF), vm((n, 4, f, rank_max), BF),
-            vm((n, 8, f, 128), BF), vm((n, 2, 2, 64, 128), BF), vm((n, 2, 2, 64, 128), BF),
-            vm((n, 2, 2, f, 128), BF), vm((n, 2, f, 128), F32), vm((n, 2, f, 128), BF),
-            vm((n, 2, 3, 32, 128), BF), vm((n, 8, f, 128), BF),
+            vm((8, f, voxels), BF), vm((n, 3, f, rank_max), BF),
+            vm((2, 4, n, 128, 128), BF), vm((2, 4, n, 128, 128), F32), vm((2, 3, n, 128, 128), BF),
+            vm((2, 4, n, 32, 128), F32), vm((2, 4, n, 32, 128), BF), vm((2, 3, n, 32, 128), BF), vm((2, 4, 4, n, 32, 128), BF),
             vm((4, f, tile_len), F32), vm((4, f, 512), BF), vm((4, f, 512), BF), vm((4, f, 512), BF),
             vm((2, 64, 512), BF), vm((2, f, 512), BF),
             vm((8, 64, f), F32), vm((8, 64, f), BF), vm((2, 4, 64, f), BF), vm((2, 8, 64, f), BF), vm((4, 64, f), BF),
             vm((20, 64, f), F32),
-            dma((8,)), dma((2,)), dma((10,)), dma((n,)), dma((n, 6)),
-            dma((1,)), dma((4,)), dma((1,)), dma((3,)), dma((1,)), dma((1,)),
+            dma((8,)), dma((2,)), dma((10,)), dma((len(GROUPS),)), dma((len(GROUPS), 4)),
+            dma((1,)), dma((4,)), dma((1,)), dma((3,)), dma((1,)), dma((1,)), pltpu.SemaphoreType.REGULAR,
         ],
         compiler_params=pltpu.CompilerParams(collective_id=0, has_side_effects=True, vmem_limit_bytes=56 << 20),
         name="step",

time: 67.2 us -> 58.9 us (0.88); the launches traced: 66.4 us -> 58.8 us
  Pallas kernels: 65.7 us -> 58.1 us
    pallas_call x1, Pallas kernels: 65.7 us -> 58.1 us  [body(): pl.pallas_call(kernel, out_shape=pltpu.VMEM((8, 64, f), F32), in_specs=[a...]
where the time goes in v3:
time: 58.9 us; the launch traced here: 58.8 us
  Pallas kernels  58.1 us (99%)
  local copies, waits for them, and re-layouts  0.71 us (1%)
    pallas_call x1, Pallas kernels, body(): pl.pallas_call(kernel, out_shape=pltpu.VMEM((8, 64, f), F32), in_specs=[a...  58.1 us

profile of v3, /device:TPU:0, one launch (start us, length us, event | category | flops | bytes accessed | tf_op | source)
XLA Modules:
  0.0 58.8 jit_solution(17891294049472942637)
XLA Ops:
  0.0 58.1 %step.1 = f32[8,64,128]{2,1,0:T(8,128)S(1)} custom-call(f32[512,128]{1,0:T(8,128)} %bitcast.6, bf16[5,4,1024,256]{3,2,1,0:T(8,128)(2,1)} %u_hbm.1, bf16[5,4,1024,256]{3,2,1,0:T(8,128)(2,1)} %v_hbm.1, s32[4,5]{1,0:T(4,128)} %bitcast.7, bf16[5,2,4,128,128]{4,3,2,1,0:T(8,128)(2,1)} %bitcast.5), custom_call_target="tpu_custom_call" | custom-call | tf_op jit(solution)/shard_map/step/pallas_call | solution.py:424
  58.1 0.7 %copy.7 = f32[4,2,64,128]{3,2,1,0:T(8,128)} copy(f32[4,2,64,128]{3,2,1,0:T(8,128)S(1)} %bitcast.4) | data formatting | bytes 524288

commit v4 on v3

--- a/solution.py
+++ b/solution.py
@@ -50,7 +50,7 @@
     img_hbm, u_hbm, v_hbm, ranks_hbm, meas_hbm, out,
     ranks, img, u, v, mb, mt, xt, coef,
     ps, kept, r1, sums, ph2, r2, rt,
-    grad, cs, cr, zs, zd, zr, moved, m16, hr, hc, hx, s1,
+    grad, cs, cr, zs, zd, zr, moved, m16, hr, hc, hx, s1, pre,
     lsem, ax_s, ax_r, ex_s, ex_r, gc_s, gc_r, gz_s, gz_r, hs_s, hs_r, ready,
 ):
     n_i = u.shape[0]
@@ -90,13 +90,6 @@
         pl.semaphore_signal(barrier, inc=1, device_id=peer, device_id_type=MESH)
 
     img_copy.wait()
-    v_copies[0].start()
-    for k in (1, 2, 3):
-        v_copies[k].start()
-    for m in m_copies:
-        m.start()
-    for k in range(4):
-        u_copies[k].start()
     xt[r] = img[...].T.astype(BF)
     pl.semaphore_wait(barrier, len(peers))
     for peer in sides:
@@ -121,6 +114,12 @@
     whole = (xt, 0)
     for i in (1, 2, 0):
         out_x[i].start()
+    for k in range(4):
+        v_copies[k].start()
+    for m in m_copies:
+        m.start()
+    for k in range(4):
+        u_copies[k].start()
     arrived(whole, (ax_s, 1))
     for i in (3, 4):
         out_x[i].start()
@@ -233,8 +232,8 @@
                 part = sums[ax, 0, i]
                 for d in range(3):
                     part += r2[ax, d, i].astype(F32)
-                rt[ax, p, s, i] = (part - mt[i, ax, pl.ds(pl.multiple_of(s * 32, 32), 32)]).astype(BF)
-            mine = (rt, ax, p, s, tiles)
+                rt[ax, p, i, s] = (part - mt[i, ax, pl.ds(pl.multiple_of(s * 32, 32), 32)]).astype(BF)
+            mine = (rt, ax, p, first, s)
             for d in (2, 1, 3):
                 send(g, 2, mine, mine, dev2((s + d) % 4))
 
@@ -246,7 +245,7 @@
         for d in (2, 1, 3):
             for ax in (0, 1):
                 p, dev1, s, dev2 = axes[ax]
-                mine = (rt, ax, p, slice(None), tiles)
+                mine = (rt, ax, p, first)
                 send(g, 3, mine, mine, dev1((p + d) % 4))
 
     def landed(g):
@@ -255,7 +254,7 @@
         arrived((r1, every, every, pl.ds(first, count)), (ex_r, g, 3))
 
     def back(i, k):
-        res = jnp.concatenate([rt[q // 4, q % 4, :, i].reshape(128, 128) for q in range(8)], axis=1)
+        res = jnp.concatenate([rt[q // 4, q % 4, i].reshape(128, 128) for q in range(8)], axis=1)
         return masked(jnp.dot(res, u[i, k], preferred_element_type=F32), i, k)
 
     def adjoint(g, k):
@@ -335,6 +334,18 @@
     for n in (4, 5, 6, 7, 0, 1, 2, 3):
         hsend[n].start()
 
+    zrow = lax.broadcasted_iota(jnp.int32, (64, 128), 0)
+
+    def along_z(center):
+        up = jnp.where(zrow == 63, 0.0, pltpu.roll(center, 63, 0))
+        fz = flux(up - center)
+        down = -pltpu.roll(fz, 1, 0)
+        first8 = jnp.where(zrow[:8] == 0, flux(-center[:8]), down[:8])
+        return fz + jnp.concatenate([first8, down[8:]], axis=0)
+
+    for n in range(8):
+        pre[n] = along_z(moved[n])
+
     arrived((xt, pl.ds(0, 6)), (ax_s, 0))
     arrived(cs, (gc_s, 0))
     arrived((zs, pl.ds(0, 3)), (gz_s, 0))
@@ -344,7 +355,6 @@
 
     has = {-1: r > 0, 4: r < 7}
     hasc = {-1: c > 0, 2: c < 15}
-    zrow = lax.broadcasted_iota(jnp.int32, (64, 128), 0)
 
     def inside(a, b):
         conds = []
@@ -377,7 +387,7 @@
             return s1[8 + b if a < 0 else 10 + b]
         return s1[12 + a if b < 0 else 16 + a]
 
-    def diffuse(source, cells, store):
+    def diffuse(source, cells, store, early):
         fx, fy = {}, {}
 
         def edge(table, a, b, da, db):
@@ -387,12 +397,8 @@
 
         for a, b in cells:
             center = source(a, b)
-            up = jnp.where(zrow == 63, 0.0, pltpu.roll(center, 63, 0))
-            fz = flux(up - center)
-            edge0 = flux(-center)
-            down = jnp.where(zrow == 0, edge0, -pltpu.roll(fz, 1, 0))
             total = edge(fx, a, b, 1, 0) - edge(fx, a - 1, b, 1, 0) + edge(fy, a, b, 0, 1) - edge(fy, a, b - 1, 0, 1)
-            total = total + fz + down
+            total = total + (pre[2 * a + b] if early and 0 <= a <= 3 and 0 <= b <= 1 else along_z(center))
             store(a, b, center + 0.12 * total)
 
     def store1(a, b, value):
@@ -408,8 +414,8 @@
 
     own_cells = [(a, b) for a in range(4) for b in (0, 1)]
     cells1 = [(a, b) for a in range(-1, 5) for b in range(-1, 3) if 0 <= a <= 3 or 0 <= b <= 1]
-    diffuse(first, cells1, store1)
-    diffuse(second, own_cells, store2)
+    diffuse(first, cells1, store1, True)
+    diffuse(second, own_cells, store2, False)
     arrived((v, 0, 0, pl.ds(0, 896)), (hs_s, 0))
 
 
@@ -432,11 +438,11 @@
             vm((2, n, 128, f), BF), vm((n, 2, f, 128), F32),
             vm((8, f, voxels), BF), vm((n, 3, f, rank_max), BF),
             vm((2, 4, n, 128, 128), BF), vm((2, 4, n, 128, 128), F32), vm((2, 3, n, 128, 128), BF),
-            vm((2, 4, n, 32, 128), F32), vm((2, 4, n, 32, 128), BF), vm((2, 3, n, 32, 128), BF), vm((2, 4, 4, n, 32, 128), BF),
+            vm((2, 4, n, 32, 128), F32), vm((2, 4, n, 32, 128), BF), vm((2, 3, n, 32, 128), BF), vm((2, 4, n, 4, 32, 128), BF),
             vm((4, f, tile_len), F32), vm((4, f, 512), BF), vm((4, f, 512), BF), vm((4, f, 512), BF),
             vm((2, 64, 512), BF), vm((2, f, 512), BF),
             vm((8, 64, f), F32), vm((8, 64, f), BF), vm((2, 4, 64, f), BF), vm((2, 8, 64, f), BF), vm((4, 64, f), BF),
-            vm((20, 64, f), F32),
+            vm((20, 64, f), F32), vm((8, 64, f), F32),
             dma((8,)), dma((2,)), dma((10,)), dma((len(GROUPS),)), dma((len(GROUPS), 4)),
             dma((1,)), dma((4,)), dma((1,)), dma((3,)), dma((1,)), dma((1,)), pltpu.SemaphoreType.REGULAR,
         ],

time: 58.9 us -> 59 us (level)
  no operation moved by 1% of the time
where the time goes in v4:
time: 59 us; the launch traced here: 58.9 us
  Pallas kernels  58.2 us (99%)
  local copies, waits for them, and re-layouts  0.71 us (1%)
    pallas_call x1, Pallas kernels, body(): pl.pallas_call(kernel, out_shape=pltpu.VMEM((8, 64, f), F32), in_specs=[a...  58.2 us

profile of v4, /device:TPU:0, one launch (start us, length us, event | category | flops | bytes accessed | tf_op | source)
XLA Modules:
  0.0 58.9 jit_solution(13831877034404806198)
XLA Ops:
  0.0 58.2 %step.1 = f32[8,64,128]{2,1,0:T(8,128)S(1)} custom-call(f32[512,128]{1,0:T(8,128)} %bitcast.6, bf16[5,4,1024,256]{3,2,1,0:T(8,128)(2,1)} %u_hbm.1, bf16[5,4,1024,256]{3,2,1,0:T(8,128)(2,1)} %v_hbm.1, s32[4,5]{1,0:T(4,128)} %bitcast.7, bf16[5,2,4,128,128]{4,3,2,1,0:T(8,128)(2,1)} %bitcast.5), custom_call_target="tpu_custom_call" | custom-call | tf_op jit(solution)/shard_map/step/pallas_call | solution.py:430
  58.2 0.7 %copy.7 = f32[4,2,64,128]{3,2,1,0:T(8,128)} copy(f32[4,2,64,128]{3,2,1,0:T(8,128)S(1)} %bitcast.4) | data formatting | bytes 524288

commit v5 on v4

--- a/solution.py
+++ b/solution.py
@@ -331,7 +331,7 @@
         Copy((m16, 1), (hx, 2), (hs_s, 0), (hs_r, 0), (rm, cp)),
         Copy((m16, 0), (hx, 3), (hs_s, 0), (hs_r, 0), (rm, cm)),
     ]
-    for n in (4, 5, 6, 7, 0, 1, 2, 3):
+    for n in (4, 5, 6, 7, 2, 3, 0, 1):
         hsend[n].start()
 
     zrow = lax.broadcasted_iota(jnp.int32, (64, 128), 0)

time: 59 us -> 59 us (level)
  no operation moved by 1% of the time
where the time goes in v5:
time: 59 us; the launch traced here: 58.9 us
  Pallas kernels  58.2 us (99%)
  local copies, waits for them, and re-layouts  0.71 us (1%)
    pallas_call x1, Pallas kernels, body(): pl.pallas_call(kernel, out_shape=pltpu.VMEM((8, 64, f), F32), in_specs=[a...  58.2 us

profile of v5, /device:TPU:0, one launch (start us, length us, event | category | flops | bytes accessed | tf_op | source)
XLA Modules:
  0.0 58.9 jit_solution(12948888930795555118)
XLA Ops:
  0.0 58.2 %step.1 = f32[8,64,128]{2,1,0:T(8,128)S(1)} custom-call(f32[512,128]{1,0:T(8,128)} %bitcast.6, bf16[5,4,1024,256]{3,2,1,0:T(8,128)(2,1)} %u_hbm.1, bf16[5,4,1024,256]{3,2,1,0:T(8,128)(2,1)} %v_hbm.1, s32[4,5]{1,0:T(4,128)} %bitcast.7, bf16[5,2,4,128,128]{4,3,2,1,0:T(8,128)(2,1)} %bitcast.5), custom_call_target="tpu_custom_call" | custom-call | tf_op jit(solution)/shard_map/step/pallas_call | solution.py:430
  58.2 0.7 %copy.7 = f32[4,2,64,128]{3,2,1,0:T(8,128)} copy(f32[4,2,64,128]{3,2,1,0:T(8,128)S(1)} %bitcast.4) | data formatting | bytes 524288
